TPU v7x, 32 devices: a whole 2x2x4 slice. The times are simulated.
32 devices in a mesh: group: 2 (over x), tp: 16 (over z, y, core).
Axes of the slice: x: 2, y: 2, z: 4, core: 2. Of those that a mesh axis runs over, the one named last changes fastest.
Arguments:
- hidden_in: bfloat16 [256, 12288], P(('group', 'tp')), parts along dimension 0, may hold values from -6 to 6
- norm_gain: float32 [12288], replicated, may hold values from 0.1 to 1.9
- norm_shift: float32 [12288], replicated, may hold values from -3 to 3
- up_weight: bfloat16 [12288, 32768], P(None, 'tp'), may hold values from -0.0546875 to 0.0546875
- up_bias: bfloat16 [32768], P('tp'), may hold values from -3 to 3
- down_weight: bfloat16 [32768, 12288], P('tp'), may hold values from -0.09375 to 0.09375
- down_bias: float32 [12288], replicated, may hold values from -3 to 3
- active: int32 [256, 32], P(('group', 'tp')), parts along dimension 0, may hold values from 0 to 255, all different within a row; in each aligned block of 8 rows (0 to 7, 8 to 15, ...) at most 2 rows name the same one
Outputs:
- mixed: bfloat16 [256, 12288], P(('group', 'tp')), parts along dimension 0
There are 2 independent parts, one for each index of `group`. A program takes and returns all parts, laid end to end along the dimension named above; an argument that names none is the same for every part. Nothing has to cross between parts.
Inputs may be any that keep to these rules, and one draw needn't show every extreme that they name: `active`: each row names 32 different blocks; among the 8 rows of one device no block is named by more than 2 rows, and some block is named by exactly 2 of them.
All inputs are finite; a program needn't handle non-finite values.
Results may differ from a plain program's by a relative error of at most 0.0075.
Values may be sent and summed in bfloat16 or wider, within the bound.
A program may use at most 256 MiB of HBM per device.

v0:
```python
import jax
import jax.numpy as jnp
from jax import lax
from jax.sharding import PartitionSpec as P

BLOCK = 128


def layer_norm(hidden_in, norm_gain, norm_shift):
    values = hidden_in.astype(jnp.float32)
    center = jnp.mean(values, axis=1, keepdims=True)
    spread = jnp.mean((values - center) ** 2, axis=1, keepdims=True)
    scaled = (values - center) / jnp.sqrt(spread + 1e-05)
    return (scaled * norm_gain + norm_shift).astype(jnp.bfloat16)


def per_device(
    hidden_in, norm_gain, norm_shift, up_weight, up_bias, down_weight, down_bias, active
):
    local_blocks = up_weight.shape[1] // BLOCK
    normed = layer_norm(hidden_in, norm_gain, norm_shift)
    rows = lax.all_gather(normed, "tp", axis=0, tiled=True)
    ids = lax.all_gather(active, "tp", axis=0, tiled=True)
    own = lax.axis_index("tp") * local_blocks + jnp.arange(local_blocks, dtype=jnp.int32)
    mask = jnp.any(ids[:, :, None] == own[None, None, :], axis=1)
    preact = jnp.dot(rows, up_weight, preferred_element_type=jnp.float32)
    preact = preact + up_bias.astype(jnp.float32)
    activated = jnp.maximum(preact, 0.0).astype(jnp.bfloat16)
    activated = jnp.where(jnp.repeat(mask, BLOCK, axis=1), activated, 0)
    part = jnp.dot(activated, down_weight, preferred_element_type=jnp.float32)
    summed = lax.psum_scatter(part.astype(jnp.bfloat16), "tp", scatter_dimension=0, tiled=True)
    return (summed.astype(jnp.float32) + down_bias).astype(jnp.bfloat16)


def solution(mesh):
    return jax.shard_map(
        per_device,
        mesh=mesh,
        in_specs=(
            P(("group", "tp"), None),
            P(),
            P(),
            P(None, "tp"),
            P("tp"),
            P("tp", None),
            P(),
            P(("group", "tp"), None),
        ),
        out_specs=P(("group", "tp"), None),
        check_vma=False,
    )
```

profile of v0, /device:TPU:0, one launch (start us, length us, event | category | flops | bytes accessed | tf_op | source)
XLA Modules:
  0.0 172.1 jit_solution(13958404057983531524)
XLA Ops:
  6.5 0.0 all-gather.2.cloned.1.call-start
  6.5 1.1 convert_reduce_fusion
  7.7 1.2 fusion.9
  8.9 1.8 %fusion.12 = bf16[8,12288]{1,0:T(8,128)(2,1)} fusion(bf16[8,12288]{1,0:T(8,128)(2,1)} %param.8, f32[12288]{0:T(1024)} %param.10, f32[12288]{0:T(1024)} %param.9, f32[8]{0:T(128)S(1)} %add_sqrt_fusion, f32[8]{0:T(128)S(1)} %broadcast_multiply_fusion), kind=kLoop, calls=%fused_computation.16 | loop fusion | flops 589824 | bytes 491584 | tf_op jit(solution)/shard_map/convert_element_type | solution.py:14
  10.7 0.0 all-gather.2.cloned.1.call-update
  10.7 0.0 reduce-scatter.2.cloned.1.call-start
  10.8 0.7 convert_element_type.25
  11.5 23.7 %all_gather.6 = s32[128,32]{1,0:T(8,128)S(1)} all-gather(s32[8,32]{1,0:T(8,128)} %param.15), channel_id=1, replica_groups=mesh['group'=2,'tp'=16] {'tp'}, dimensions={0}, use_global_device_ids=true | all-gather | bytes 17408 | tf_op jit(solution)/shard_map/all_gather | solution.py:23
  35.1 0.1 copy.9
  35.2 0.1 compare_reduce_fusion
  35.3 0.1 copy.10
  35.4 23.4 %all-gather.2.cloned.1.call-done = bf16[128,12288]{1,0:T(8,128)(2,1)} async-done(((bf16[8,12288]{1,0:T(8,128)(2,1)}), bf16[128,12288]{1,0:T(8,128)(2,1)}) %all-gather.2.cloned.1.call-update) | async-done | bytes 3145744 | tf_op jit(solution)/shard_map/all_gather | solution.py:22
  58.9 0.3 broadcast_in_dim.5
  59.2 0.0 copy-start
  59.2 19.7 %fusion.2.clone.4 = bf16[128,2048]{1,0:T(8,128)(2,1)S(1)} fusion(bf16[128,12288]{1,0:T(8,128)(2,1)} %all-gather.2.cloned.1.call-done, bf16[12288,2048]{1,0:T(8,128)(2,1)} %param.11, pred[16,8,16,128]{3,2,1,0:T(8,128)(4,1)S(1)} %bitcast.20, f32[2048]{0:T(1024)S(1)} %convert_element_type.25), kind=kOutput, calls=%fused_computation.4.clone.clone.clone.1 | convolution fusion | flops 6443499520 | bytes 54272000 | tf_op jit(solution)/shard_map/dot_general | solution.py:26
  79.0 19.5 %convolution_convert_fusion = bf16[128,12288]{1,0:T(8,128)(2,1)} fusion(bf16[2048,12288]{1,0:T(8,128)(2,1)} %param.13, bf16[128,2048]{1,0:T(8,128)(2,1)S(1)} %fusion.2.clone.4), kind=kOutput, calls=%fused_computation | convolution fusion | flops 6444023808 | bytes 54001664 | tf_op jit(solution)/shard_map/dot_general | solution.py:30
  98.5 0.0 reduce-scatter.2.cloned.1.call-update
  98.5 65.2 %reduce-scatter.2.cloned.1.call-done = bf16[8,12288]{1,0:T(8,128)(2,1)} async-done(((bf16[128,12288]{1,0:T(8,128)(2,1)}), bf16[8,12288]{1,0:T(8,128)(2,1)}) %reduce-scatter.2.cloned.1.call-update) | async-done | bytes 196624 | tf_op jit(solution)/shard_map/reduce_scatter | solution.py:31
  163.7 0.0 copy-done
  163.7 1.6 add_convert_fusion
  (3 shorter events, 0.0 us)
Async XLA Ops:
  6.5 52.3 %all-gather.2.cloned.1.call-start = ((), (), s32[]{:S(2)}) async-start(), calls=%async_computation.1 | async-start | bytes 3342336 | tf_op jit(solution)/shard_map/all_gather | solution.py:22
  10.7 152.9 %reduce-scatter.2.cloned.1.call-start = ((), (), s32[]{:S(2)}) async-start(), calls=%async_computation.2 | async-start | bytes 3342336 | tf_op jit(solution)/shard_map/reduce_scatter | solution.py:31
  59.2 104.4 %copy-start = (f32[12288]{0:T(1024)S(1)}, f32[12288]{0:T(1024)}, u32[]{:S(2)}) copy-start(f32[12288]{0:T(1024)} %param.14) | copy-start | bytes 147460
Sparse Core Ops, SparseCore 0:
  10.8 48.0 all-gather.1
  98.6 65.0 reduce-scatter.1
where the time goes:
time: 172 us
  waiting for transfers between devices  88.7 us (52%)
  matrix products  39.2 us (23%)
  blocking collectives  23.7 us (14%)
  between operations  13.4 us (8%)
  other arithmetic  6.61 us (4%)
    reduce_scatter x1, waiting for transfers between devices, per_device(): lax.psum_scatter(part.astype(jnp.bfloat16), 'tp', scatter_dimension=0, ti...  65.2 us
    all_gather x1, blocking collectives, per_device(): ids = lax.all_gather(active, 'tp', axis=0, tiled=True)  23.7 us
    all_gather x1, waiting for transfers between devices, per_device(): rows = lax.all_gather(normed, 'tp', axis=0, tiled=True)  23.4 us
    dot_general x1, matrix products, per_device(): preact = jnp.dot(rows, up_weight, preferred_element_type=jnp.float32)  19.7 us
    dot_general x1, matrix products, per_device(): part = jnp.dot(activated, down_weight, preferred_element_type=jnp.float32)  19.5 us
  transfers between devices with their start and end apart: 2, of which 2 were waited for; matrix products, arithmetic and copies ran while one was open for 1% of the time, Pallas kernels for 0%

commit v1 on v0

--- a/solution.py
+++ b/solution.py
@@ -1,6 +1,10 @@
+import functools
+
 import jax
 import jax.numpy as jnp
 from jax import lax
+from jax.experimental import pallas as pl
+from jax.experimental.pallas import tpu as pltpu
 from jax.sharding import PartitionSpec as P
 
 BLOCK = 128
@@ -14,7 +18,354 @@
     return (scaled * norm_gain + norm_shift).astype(jnp.bfloat16)
 
 
-def per_device(
+F32 = jnp.float32
+BF16 = jnp.bfloat16
+SLOTS = 10
+
+
+def fused_kernel(
+    dims, hidden, gain, shift, up_hbm, up_bias, down_hbm, down_bias, active, out,
+    wbuf, xn, xs, ids_own, ids_sib, xg, idg, preact, act, part, pown,
+    ssend, srecv, asend, arecv, bsend, brecv,
+    w_sem, e_send, e_recv, ga_send, ga_recv, gb_send, gb_recv, gs_send, gs_recv,
+    ia_send, ia_recv, ib_send, ib_recv, ra_send, ra_recv, rb_send, rb_recv, rs_send, rs_recv,
+):
+    chips, chunks, wide, slots = dims
+    half = wide // 2
+    hops_a, hops_b = chips // 2, chips - 1 - chips // 2
+    deep = chips // 2
+    me = lax.axis_index("tp")
+    core = lax.rem(me, 2)
+    chip = me // 2
+    side = lax.rem(chip, 2)
+    step_z = chip // 2
+    pos = step_z + side * (2 * deep - 1 - 2 * step_z)
+    turn = 1 - 2 * core
+
+    def device_at(place):
+        s = place // deep
+        z = place + s * (2 * deep - 1 - 2 * place)
+        return (z * 2 + s) * 2 + core
+
+    def place_of(offset):
+        return lax.rem(pos + turn * offset + 2 * chips, chips)
+
+    to_a = device_at(place_of(1))
+    to_b = device_at(place_of(-1))
+    sibling = chip * 2 + 1 - core
+
+    def send(src, dst, s_sem, r_sem, target):
+        return pltpu.make_async_remote_copy(
+            src_ref=src, dst_ref=dst, send_sem=s_sem, recv_sem=r_sem,
+            device_id={"tp": target}, device_id_type=pl.DeviceIdType.MESH,
+        )
+
+    def block(place):
+        return pl.ds(pl.multiple_of(place * 16, 16), 16)
+
+    def w_up(g, slot, j):
+        rows = pl.ds(pl.multiple_of(g * wide, wide), wide)
+        return pltpu.make_async_copy(
+            up_hbm.at[rows, pl.ds(j * wide, wide)],
+            wbuf.at[slot, :, pl.ds(j * wide, wide)], w_sem.at[slot, j])
+
+    def w_down(n, slot, j):
+        cols = pl.ds(pl.multiple_of(n * wide, wide), wide)
+        return pltpu.make_async_copy(
+            down_hbm.at[pl.ds(j * wide, wide), cols],
+            wbuf.at[slot, :, pl.ds(j * wide, wide)], w_sem.at[slot, j])
+
+    def w_start(g):
+        slot = lax.rem(g, slots)
+
+        @pl.when(g < chunks)
+        def _():
+            w_up(g, slot, 0).start()
+            w_up(g, slot, 1).start()
+
+        @pl.when((g >= chunks) & (g < 2 * chunks))
+        def _():
+            w_down(g - chunks, slot, 0).start()
+            w_down(g - chunks, slot, 1).start()
+
+    for g in range(slots):
+        for j in range(2):
+            w_up(g, g, j).start()
+
+    barrier = pltpu.get_barrier_semaphore()
+    for other in (to_a, to_b, sibling):
+        pl.semaphore_signal(
+            barrier, inc=1, device_id={"tp": other}, device_id_type=pl.DeviceIdType.MESH)
+
+    values = hidden[...].astype(F32)
+    center = jnp.mean(values, axis=1, keepdims=True)
+    spread = jnp.mean((values - center) ** 2, axis=1, keepdims=True)
+    root = jnp.sqrt(spread + 1e-05)
+    for k in range(chunks):
+        for h in range(2):
+            cols = slice(k * wide + h * half, k * wide + h * half + half)
+            scaled = (hidden[:, cols].astype(F32) - center) / root
+            xn[h, k] = (scaled * gain[:, cols] + shift[:, cols]).astype(BF16).astype(F32)
+    ids_own[...] = jnp.full(ids_own.shape, -1.0, F32)
+    ids_own[:, : active.shape[1]] = active[...].astype(F32)
+    preact[...] = jnp.zeros(preact.shape, F32)
+    pl.semaphore_wait(barrier, 3)
+    swap_x = send(xn.at[1 - core], xs, e_send.at[0], e_recv.at[0], sibling)
+    swap_i = send(ids_own, ids_sib, e_send.at[1], e_recv.at[1], sibling)
+    swap_x.start()
+    swap_i.start()
+    swap_x.wait_recv()
+    swap_i.wait_recv()
+
+    def pair(mine, theirs):
+        first = jnp.where(core == 0, mine, theirs)
+        second = jnp.where(core == 0, theirs, mine)
+        return jnp.concatenate([first, second], axis=0).astype(BF16)
+
+    idg[block(pos), :] = pair(ids_own[...], ids_sib[...])
+
+    def g_a(k, h):
+        ref = xg.at[k, core, block(place_of(-(h - 1))), :]
+        return send(ref, ref, ga_send.at[k, h - 1], ga_recv.at[k, h - 1], to_a)
+
+    def g_b(k, h):
+        ref = xg.at[k, core, block(place_of(h - 1)), :]
+        return send(ref, ref, gb_send.at[k, h - 1], gb_recv.at[k, h - 1], to_b)
+
+    def i_a(h):
+        ref = idg.at[block(place_of(-(h - 1))), :]
+        return send(ref, ref, ia_send.at[h - 1], ia_recv.at[h - 1], to_a)
+
+    def i_b(h):
+        ref = idg.at[block(place_of(h - 1)), :]
+        return send(ref, ref, ib_send.at[h - 1], ib_recv.at[h - 1], to_b)
+
+    def g_s(k):
+        ref = xg.at[k, core]
+        return send(ref, ref, gs_send.at[k], gs_recv.at[k], sibling)
+
+    def gather_step(s, carry):
+        @pl.when(s < chunks)
+        def _():
+            xg[s, core, block(pos), :] = pair(xn[core, s], xs[s])
+            g_a(s, 1).start()
+            g_b(s, 1).start()
+
+        @pl.when(s == 0)
+        def _():
+            i_a(1).start()
+            i_b(1).start()
+
+        for h in range(1, hops_a + 1):
+            k = s - h
+
+            @pl.when((k >= 0) & (k < chunks))
+            def _():
+                g_a(k, h).wait_recv()
+                if h < hops_a:
+                    g_a(k, h + 1).start()
+                if h <= hops_b:
+                    g_b(k, h).wait_recv()
+                if h < hops_b:
+                    g_b(k, h + 1).start()
+                if h == hops_a:
+                    g_s(k).start()
+
+            @pl.when(k == 0)
+            def _():
+                i_a(h).wait_recv()
+                if h < hops_a:
+                    i_a(h + 1).start()
+                if h <= hops_b:
+                    i_b(h).wait_recv()
+                if h < hops_b:
+                    i_b(h + 1).start()
+
+        k = s - hops_a - 1
+
+        @pl.when(k >= 0)
+        def _():
+            g_s(k).wait_recv()
+            slot = lax.rem(k, slots)
+            w_up(k, slot, 0).wait()
+            w_up(k, slot, 1).wait()
+            tile = min(512, wide)
+            for j in range(0, 2 * wide, tile):
+                cols = slice(j, j + tile)
+                preact[:, cols] += jnp.dot(
+                    xg[k, 0], wbuf[slot, :half, cols], preferred_element_type=F32
+                ) + jnp.dot(xg[k, 1], wbuf[slot, half:, cols], preferred_element_type=F32)
+            w_start(k + slots)
+
+        return carry
+
+    lax.fori_loop(0, chunks + hops_a + 1, gather_step, 0)
+
+    ids = idg[...].astype(F32)
+    for b in range(2 * wide // BLOCK):
+        cols = slice(b * BLOCK, b * BLOCK + BLOCK)
+        name = (me * (2 * wide // BLOCK) + b).astype(F32)
+        named = jnp.max(jnp.where(ids == name, 1.0, 0.0), axis=1, keepdims=True)
+        value = jnp.maximum(preact[:, cols] + up_bias[:, cols].astype(F32), 0.0)
+        act[:, cols] = (value * named).astype(BF16)
+
+    def r_s(n):
+        return send(ssend.at[n], srecv.at[n], rs_send.at[n], rs_recv.at[n], sibling)
+
+    def r_a(n, h):
+        return send(asend.at[n, h - 1], arecv.at[n, h - 1], ra_send.at[n, h - 1],
+                    ra_recv.at[n, h - 1], to_a)
+
+    def r_b(n, h):
+        return send(bsend.at[n, h - 1], brecv.at[n, h - 1], rb_send.at[n, h - 1],
+                    rb_recv.at[n, h - 1], to_b)
+
+    def scatter_step(s, carry):
+        n = s - hops_a - 1
+
+        @pl.when(n >= 0)
+        def _():
+            r_a(n, hops_a).wait_recv()
+            r_b(n, hops_b).wait_recv()
+            total = pown[n, block(pos), :] + arecv[n, hops_a - 1].astype(F32)
+            total = total + brecv[n, hops_b - 1].astype(F32)
+            for h in range(2):
+                cols = pl.ds(pl.multiple_of(n * wide + h * half, half), half)
+                out[:, cols] = (total[8 * h : 8 * h + 8] + down_bias[:, cols]).astype(BF16)
+
+        for h in range(hops_a - 1, 0, -1):
+            n = s - 1 - h
+
+            @pl.when((n >= 0) & (n < chunks))
+            def _():
+                r_a(n, h).wait_recv()
+                here = pown[n, block(place_of(hops_a - h)), :]
+                asend[n, h] = (arecv[n, h - 1].astype(F32) + here).astype(BF16)
+                r_a(n, h + 1).start()
+                if h < hops_b:
+                    r_b(n, h).wait_recv()
+                    here = pown[n, block(place_of(h - hops_b)), :]
+                    bsend[n, h] = (brecv[n, h - 1].astype(F32) + here).astype(BF16)
+                    r_b(n, h + 1).start()
+
+        n = s - 1
+
+        @pl.when((n >= 0) & (n < chunks))
+        def _():
+            r_s(n).wait_recv()
+            pown[n] = pown[n] + srecv[n].astype(F32)
+            asend[n, 0] = pown[n, block(place_of(hops_a)), :].astype(BF16)
+            r_a(n, 1).start()
+            bsend[n, 0] = pown[n, block(place_of(-hops_b)), :].astype(BF16)
+            r_b(n, 1).start()
+
+        @pl.when(s < chunks)
+        def _():
+            slot = lax.rem(s + chunks, slots)
+            w_down(s, slot, 0).wait()
+            w_down(s, slot, 1).wait()
+            tile = min(512, wide)
+            for j in range(0, wide, tile):
+                part[:, j : j + tile] = jnp.dot(
+                    act[:, :wide], wbuf[slot, :, j : j + tile], preferred_element_type=F32
+                ) + jnp.dot(
+                    act[:, wide:], wbuf[slot, :, wide + j : wide + j + tile],
+                    preferred_element_type=F32)
+            w_start(s + chunks + slots)
+            for p in range(chips):
+                theirs = part[pl.ds(pl.multiple_of(p * 16 + 8 - 8 * core, 8), 8), :]
+                mine = part[pl.ds(pl.multiple_of(p * 16 + 8 * core, 8), 8), :]
+                rows = slice(p * 16, p * 16 + 16)
+                ssend[s, rows, :] = jnp.concatenate(
+                    [theirs[:, :half], theirs[:, half:]], axis=0).astype(BF16)
+                pown[s, rows, :] = jnp.concatenate([mine[:, :half], mine[:, half:]], axis=0)
+            r_s(s).start()
+
+        return carry
+
+    lax.fori_loop(0, chunks + hops_a + 1, scatter_step, 0)
+
+    swap_x.wait_send()
+    swap_i.wait_send()
+    for h in range(1, hops_a + 1):
+        i_a(h).wait_send()
+    for h in range(1, hops_b + 1):
+        i_b(h).wait_send()
+
+    def drain(k, carry):
+        g_s(k).wait_send()
+        r_s(k).wait_send()
+        for h in range(1, hops_a + 1):
+            g_a(k, h).wait_send()
+            r_a(k, h).wait_send()
+        for h in range(1, hops_b + 1):
+            g_b(k, h).wait_send()
+            r_b(k, h).wait_send()
+        return carry
+
+    lax.fori_loop(0, chunks, drain, 0)
+
+
+def fused(hidden_in, norm_gain, norm_shift, up_weight, up_bias, down_weight, down_bias, active):
+    members = lax.axis_size("tp")
+    rows, features = hidden_in.shape
+    neurons = up_weight.shape[1]
+    chips = members // 2
+    wide = neurons // 2
+    half = wide // 2
+    chunks = features // wide
+    slots = min(SLOTS, chunks)
+    hops_a, hops_b = chips // 2, chips - 1 - chips // 2
+    everyone = members * rows
+    vmem = pl.BlockSpec(memory_space=pltpu.VMEM)
+    hbm = pl.BlockSpec(memory_space=pl.ANY)
+    dma = pltpu.SemaphoreType.DMA
+    return pl.pallas_call(
+        functools.partial(fused_kernel, (chips, chunks, wide, slots)),
+        out_shape=jax.ShapeDtypeStruct((rows, features), BF16),
+        in_specs=[vmem, vmem, vmem, hbm, vmem, hbm, vmem, vmem],
+        out_specs=vmem,
+        scratch_shapes=[
+            pltpu.VMEM((slots, wide, 2 * wide), BF16),
+            pltpu.VMEM((2, chunks, rows, half), F32),
+            pltpu.VMEM((chunks, rows, half), F32),
+            pltpu.VMEM((rows, 128), F32),
+            pltpu.VMEM((rows, 128), F32),
+            pltpu.VMEM((chunks, 2, everyone, half), BF16),
+            pltpu.VMEM((everyone, 128), BF16),
+            pltpu.VMEM((everyone, neurons), F32),
+            pltpu.VMEM((everyone, neurons), BF16),
+            pltpu.VMEM((everyone, wide), F32),
+            pltpu.VMEM((chunks, everyone, half), F32),
+            pltpu.VMEM((chunks, everyone, half), BF16),
+            pltpu.VMEM((chunks, everyone, half), BF16),
+            pltpu.VMEM((chunks, hops_a, 16, half), BF16),
+            pltpu.VMEM((chunks, hops_a, 16, half), BF16),
+            pltpu.VMEM((chunks, hops_b, 16, half), BF16),
+            pltpu.VMEM((chunks, hops_b, 16, half), BF16),
+            dma((slots, 2)),
+            dma((2,)), dma((2,)),
+            dma((chunks, hops_a)), dma((chunks, hops_a)),
+            dma((chunks, hops_b)), dma((chunks, hops_b)),
+            dma((chunks,)), dma((chunks,)),
+            dma((hops_a,)), dma((hops_a,)), dma((hops_b,)), dma((hops_b,)),
+            dma((chunks, hops_a)), dma((chunks, hops_a)),
+            dma((chunks, hops_b)), dma((chunks, hops_b)),
+            dma((chunks,)), dma((chunks,)),
+        ],
+        compiler_params=pltpu.CompilerParams(
+            collective_id=0, has_side_effects=True, vmem_limit_bytes=60 * 1024 * 1024),
+        cost_estimate=pl.CostEstimate(
+            flops=4 * everyone * features * neurons,
+            bytes_accessed=4 * features * neurons, transcendentals=0),
+        name="fused_ffn",
+    )(
+        hidden_in, norm_gain.reshape(1, -1), norm_shift.reshape(1, -1), up_weight,
+        up_bias.reshape(1, -1), down_weight, down_bias.reshape(1, -1), active,
+    )
+
+
+def plain(
     hidden_in, norm_gain, norm_shift, up_weight, up_bias, down_weight, down_bias, active
 ):
     local_blocks = up_weight.shape[1] // BLOCK
@@ -30,6 +381,22 @@
     part = jnp.dot(activated, down_weight, preferred_element_type=jnp.float32)
     summed = lax.psum_scatter(part.astype(jnp.bfloat16), "tp", scatter_dimension=0, tiled=True)
     return (summed.astype(jnp.float32) + down_bias).astype(jnp.bfloat16)
+
+
+def per_device(*operands):
+    hidden_in, up_weight, active = operands[0], operands[3], operands[7]
+    features, neurons = up_weight.shape
+    members = lax.axis_size("tp")
+    fits = (
+        members == 16
+        and hidden_in.shape[0] == 8
+        and active.shape[1] <= 128
+        and members * neurons // BLOCK <= 256
+        and neurons % 512 == 0
+        and features % (neurons // 2) == 0
+        and neurons <= 2048
+    )
+    return fused(*operands) if fits else plain(*operands)
 
 
 def solution(mesh):

time: 172 us -> 98.6 us (0.57)
  Pallas kernels: 0 us -> 95.5 us
  waiting for transfers between devices: 88.7 us -> 0 us
  matrix products: 39.2 us -> 0 us
  blocking collectives: 23.7 us -> 0 us
  between operations: 13.4 us -> 0.01 us
  other arithmetic: 6.61 us -> 0 us
  local copies, waits for them, and re-layouts: 0.52 us -> 2.91 us
    pallas_call x0 -> x1, Pallas kernels: none -> 95.5 us  [fused(): pl.pallas_call(functools.partial(fused_kernel, (chips, chunks, wide, slot...]
    reduce_scatter x1 -> x0, waiting for transfers between devices: 65.2 us -> none  [per_device(): lax.psum_scatter(part.astype(jnp.bfloat16), 'tp', scatter_dimension=0, ti...]
    dot_general x2 -> x0, matrix products: 39.2 us -> none  [the longest x1 19.7 us: per_device(): preact = jnp.dot(rows, up_weight, preferred_element_type=jnp.float32)]
    all_gather x1 -> x0, blocking collectives: 23.7 us -> none  [per_device(): ids = lax.all_gather(active, 'tp', axis=0, tiled=True)]
    all_gather x1 -> x0, waiting for transfers between devices: 23.4 us -> none  [per_device(): rows = lax.all_gather(normed, 'tp', axis=0, tiled=True)]
    convert_element_type x3 -> x0, other arithmetic: 4.11 us -> none  [the longest x1 1.78 us: layer_norm(): return (scaled * norm_gain + norm_shift).astype(jnp.bfloat16)]
    reduce_sum x2 -> x0, other arithmetic: 2.35 us -> none  [the longest x1 1.21 us: layer_norm(): spread = jnp.mean((values - center) ** 2, axis=1, keepdims=True)]
  transfers between devices with their start and end apart: 2 -> 0, of which waited for: 2 -> 0; matrix products, arithmetic and copies ran while one was open for 1% -> 0% of each run, Pallas kernels for 0% -> 0%
where the time goes in v1:
time: 98.6 us; the launch traced here: 98.4 us
  Pallas kernels  95.5 us (97%)
  local copies, waits for them, and re-layouts  2.91 us (3%)
    pallas_call x1, Pallas kernels, fused(): pl.pallas_call(functools.partial(fused_kernel, (chips, chunks, wide, slot...  95.5 us

profile of v1, /device:TPU:0, one launch (start us, length us, event | category | flops | bytes accessed | tf_op | source)
XLA Modules:
  0.0 98.4 jit_solution(2170151107587060230)
XLA Ops:
  0.0 1.3 %reshape.14.up_bias = bf16[1,2048]{1,0:T(2,128)(2,1)} reshape(bf16[2048]{0:T(1024)(128)(2,1)} %param.12) | data formatting | bytes 8192 | tf_op jit(solution)/shard_map/reshape | solution.py:364
  1.3 95.5 %fused_ffn.1 = bf16[8,12288]{1,0:T(8,128)(2,1)} custom-call(bf16[8,12288]{1,0:T(8,128)(2,1)} %hidden.1, f32[1,12288]{1,0:T(1,128)} %bitcast.3, f32[1,12288]{1,0:T(1,128)} %bitcast.4, bf16[12288,2048]{1,0:T(8,128)(2,1)} %up_hbm.1, bf16[1,2048]{1,0:T(2,128)(2,1)} %reshape.14.up_bias, bf16[2048,12288]{1,0:T(8,128)(2,1)} %down_hbm.1, f32[1,12288]{1,0:T(1,128)} %bitcast.5, ...), custom_call_target="tpu_custom_call" | custom-call | flops 12884901888 | bytes 100663296 | tf_op jit(solution)/shard_map/fused_ffn/pallas_call | solution.py:323
  96.8 1.6 %copy.10 = bf16[8,12288]{1,0:T(8,128)(2,1)} copy(bf16[8,12288]{1,0:T(8,128)(2,1)} %fused_ffn.1) | data formatting | bytes 393216

commit v2 on v1

--- a/solution.py
+++ b/solution.py
@@ -21,6 +21,8 @@
 F32 = jnp.float32
 BF16 = jnp.bfloat16
 SLOTS = 10
+GAP = 3
+SIB = 2
 
 
 def fused_kernel(
@@ -157,7 +159,7 @@
             i_b(1).start()
 
         for h in range(1, hops_a + 1):
-            k = s - h
+            k = s - GAP * h
 
             @pl.when((k >= 0) & (k < chunks))
             def _():
@@ -181,7 +183,7 @@
                 if h < hops_b:
                     i_b(h + 1).start()
 
-        k = s - hops_a - 1
+        k = s - GAP * hops_a - SIB
 
         @pl.when(k >= 0)
         def _():
@@ -199,7 +201,7 @@
 
         return carry
 
-    lax.fori_loop(0, chunks + hops_a + 1, gather_step, 0)
+    lax.fori_loop(0, chunks + GAP * hops_a + SIB, gather_step, 0)
 
     ids = idg[...].astype(F32)
     for b in range(2 * wide // BLOCK):
@@ -221,7 +223,7 @@
                     rb_recv.at[n, h - 1], to_b)
 
     def scatter_step(s, carry):
-        n = s - hops_a - 1
+        n = s - GAP * hops_a - SIB
 
         @pl.when(n >= 0)
         def _():
@@ -234,7 +236,7 @@
                 out[:, cols] = (total[8 * h : 8 * h + 8] + down_bias[:, cols]).astype(BF16)
 
         for h in range(hops_a - 1, 0, -1):
-            n = s - 1 - h
+            n = s - SIB - GAP * h
 
             @pl.when((n >= 0) & (n < chunks))
             def _():
@@ -248,7 +250,7 @@
                     bsend[n, h] = (brecv[n, h - 1].astype(F32) + here).astype(BF16)
                     r_b(n, h + 1).start()
 
-        n = s - 1
+        n = s - SIB
 
         @pl.when((n >= 0) & (n < chunks))
         def _():
@@ -283,7 +285,7 @@
 
         return carry
 
-    lax.fori_loop(0, chunks + hops_a + 1, scatter_step, 0)
+    lax.fori_loop(0, chunks + GAP * hops_a + SIB, scatter_step, 0)
 
     swap_x.wait_send()
     swap_i.wait_send()

time: 98.6 us -> 65.3 us (0.66)
  Pallas kernels: 95.5 us -> 62.2 us
    pallas_call x1, Pallas kernels: 95.5 us -> 62.2 us  [fused(): pl.pallas_call(functools.partial(fused_kernel, (chips, chunks, wide, slot...]
where the time goes in v2:
time: 65.3 us; the launch traced here: 65.1 us
  Pallas kernels  62.2 us (95%)
  local copies, waits for them, and re-layouts  2.91 us (4%)
    pallas_call x1, Pallas kernels, fused(): pl.pallas_call(functools.partial(fused_kernel, (chips, chunks, wide, slot...  62.2 us
    unnamed x1, local copies, waits for them, and re-layouts  1.62 us

profile of v2, /device:TPU:0, one launch (start us, length us, event | category | flops | bytes accessed | tf_op | source)
XLA Modules:
  0.0 65.1 jit_solution(15540886437041013423)
XLA Ops:
  0.0 1.3 %reshape.14.up_bias = bf16[1,2048]{1,0:T(2,128)(2,1)} reshape(bf16[2048]{0:T(1024)(128)(2,1)} %param.12) | data formatting | bytes 8192 | tf_op jit(solution)/shard_map/reshape | solution.py:366
  1.3 62.2 %fused_ffn.1 = bf16[8,12288]{1,0:T(8,128)(2,1)} custom-call(bf16[8,12288]{1,0:T(8,128)(2,1)} %hidden.1, f32[1,12288]{1,0:T(1,128)} %bitcast.3, f32[1,12288]{1,0:T(1,128)} %bitcast.4, bf16[12288,2048]{1,0:T(8,128)(2,1)} %up_hbm.1, bf16[1,2048]{1,0:T(2,128)(2,1)} %reshape.14.up_bias, bf16[2048,12288]{1,0:T(8,128)(2,1)} %down_hbm.1, f32[1,12288]{1,0:T(1,128)} %bitcast.5, ...), custom_call_target="tpu_custom_call" | custom-call | flops 12884901888 | bytes 100663296 | tf_op jit(solution)/shard_map/fused_ffn/pallas_call | solution.py:325
  63.5 1.6 %copy.10 = bf16[8,12288]{1,0:T(8,128)(2,1)} copy(bf16[8,12288]{1,0:T(8,128)(2,1)} %fused_ffn.1) | data formatting | bytes 393216
